TPU v7x, 32 devices: a whole 2x2x4 slice. The times are simulated.
32 devices in a mesh: grp: 2 (over y), row: 4 (over z), col: 4 (over x, core).
Axes of the slice: x: 2, y: 2, z: 4, core: 2. Of those that a mesh axis runs over, the one named last changes fastest.
Arguments:
- mask_param: float32 [2048, 1024], P(('grp', 'row'), 'col'), parts along dimension 0, may hold values from -6 to 6
- target: bfloat16 [2048, 1024], P(('grp', 'row'), 'col'), parts along dimension 0, may hold values from 0 to 1
- kernel_modes: float32 [12, 64, 128], replicated, may hold values from -24 to 24, as said below
- kernel_weight: float32 [12], replicated, may hold values from 0.02 to 0.2
Outputs:
- healed_param: float32 [2048, 1024], P(('grp', 'row'), 'col'), parts along dimension 0
There are 2 independent parts, one for each index of `grp`. A program takes and returns all parts, laid end to end along the dimension named above; an argument that names none is the same for every part. Nothing has to cross between parts.
Inputs may be any that keep to these rules, and one draw needn't show every extreme that they name: `kernel_modes`: the response of every kernel at the zero-frequency mode (row 32, columns 32 and 96) is zero.
All inputs are finite; a program needn't handle non-finite values.
Results may differ from a plain program's by a relative error of at most 0.0095.
Values may be sent and summed in bfloat16 or wider, within the bound.
A program may use at most 64 MiB of HBM per device.

v0:
```python
import functools

import jax
import jax.numpy as jnp
import ml_dtypes
import numpy as np
from jax import lax
from jax.experimental import pallas as pl
from jax.experimental.pallas import tpu as pltpu
from jax.sharding import PartitionSpec as P

TILE = 256
MARGIN = 64
MODES = 64
KERN = 12
HALF = 128
WIN = 384
GRID = 128
PAIR = 2 * MODES

STEEPNESS = 4.0
THRESHOLD = 0.4
STEP = 16.0

MESH = pl.DeviceIdType.MESH
F32 = jnp.float32
BF16 = jnp.bfloat16

AROUND = ((1, 1), (1, -1), (-1, 1), (-1, -1), (1, 0), (-1, 0), (0, 1), (0, -1))
BACK = ((-1, -1), (-1, 0), (0, -1))
AHEAD = ((1, 1), (1, 0), (0, 1))
FIRST_AT = {-1: TILE + MARGIN, 0: MARGIN, 1: MARGIN - TILE}
SECOND_AT = {-1: TILE - MARGIN, 0: -MARGIN}


def cos_sin(places):
    places = np.asarray(places)
    frequency = np.arange(MODES) - MODES // 2
    angle = np.mod(frequency[:, None] * places[None, :], WIN) * (2.0 * np.pi / WIN)
    inside = ((places >= 0) & (places < WIN))[None, :]
    return np.where(inside, np.cos(angle), 0.0), np.where(inside, np.sin(angle), 0.0)


def tables():
    own = np.arange(TILE)

    def columns(offsets):
        parts = [cos_sin(own + offset) for offset in offsets]
        real = [np.concatenate([c.T, -s.T], 1) for c, s in parts]
        imag = [np.concatenate([s.T, c.T], 1) for c, s in parts]
        return np.concatenate(real + imag, 1)

    def rows(offsets):
        parts = [cos_sin(own + offset) for offset in offsets]
        return np.concatenate([np.concatenate([c, -s], 1) for c, s in parts], 0)

    first_at = [FIRST_AT[d] for d in (-1, 0, 1)]
    second_at = [SECOND_AT[d] for d in (-1, 0)]
    c3, s3 = cos_sin(np.arange(GRID) * (WIN // GRID))
    core_c, core_s = cos_sin(own + MARGIN)
    shift = (own + MARGIN)[:, None] / WIN - np.arange(GRID)[None, :] / GRID
    waves = np.arange(1, MODES)[:, None, None] * shift[None]
    resample = (1.0 + 2.0 * np.cos(2.0 * np.pi * waves).sum(0)) / GRID
    made = dict(
        col1=columns(first_at),
        row1=rows(first_at),
        col2=columns(second_at),
        row2=rows(second_at),
        inv3=np.block([[c3, s3], [-s3, c3]]),
        lift=np.concatenate([c3, s3], 0).T,
        up=resample,
        down=resample.T,
        adj=np.block([[c3.T, -s3.T, -s3.T, -c3.T], [s3.T, c3.T, c3.T, -s3.T]]),
        fold=np.concatenate([c3, s3], 1),
        invc=np.block([[core_c, core_s], [-core_s, core_c]]),
        rowc=np.concatenate([core_c.T, -core_s.T], 1),
    )
    held = {name: value.astype(ml_dtypes.bfloat16) for name, value in made.items()}

    def minus_half(di, dj, at):
        down_c, down_s = (t.sum(1, keepdims=True) for t in cos_sin(own + at[di]))
        over_c, over_s = (t.sum(1)[None] for t in cos_sin(own + at[dj]))
        real = down_c * over_c - down_s * over_s
        imag = -(down_c * over_s + down_s * over_c)
        return np.concatenate([real, imag], 1) * (-0.5 / (WIN * WIN))

    def empty(ways, at, states, missing):
        made = []
        for state in range(states):
            total = np.zeros((MODES, PAIR))
            for di, dj in ways:
                if missing(state, di, dj):
                    total += minus_half(di, dj, at)
            made.append(total)
        return np.stack(made).astype(np.float32)

    held["none1"] = empty(
        AROUND,
        FIRST_AT,
        16,
        lambda n, di, dj: (
            (di > 0 and n & 1) or (di < 0 and n & 2) or (dj > 0 and n & 4) or (dj < 0 and n & 8)
        ),
    )
    held["none2"] = empty(
        BACK, SECOND_AT, 4, lambda n, di, dj: (di < 0 and n & 1) or (dj < 0 and n & 2)
    )
    return held


NAMES = (
    "col1", "row1", "col2", "row2", "inv3", "lift",
    "up", "down", "adj", "fold", "invc", "rowc",
)
ABSENT = ("none1", "none2")


def dot(a, b):
    return jnp.dot(a, b, preferred_element_type=F32)


def above_half(x):
    return 0.5 * jnp.tanh(0.5 * x)


def low_half():
    return lax.broadcasted_iota(jnp.int32, (MODES, PAIR), 1) < MODES


def turned(pair):
    other = pltpu.roll(pair, MODES, 1)
    return jnp.where(low_half(), -other, other)


def spectrum_parts(wire, col, row, count):
    wide = PAIR * count
    half = dot(wire, col[...]).astype(BF16)
    stacked = jnp.concatenate([half[:, :wide], half[:, wide:]], 0)
    return dot(row[...], stacked) * (1.0 / (WIN * WIN))


def adjoint_modes(spec, goal, counted, resp_real, resp_imag, fields, tab):
    filtered = resp_real[...] * spec[None] + resp_imag[...] * turned(spec)[None]
    filtered = filtered.astype(BF16).reshape(KERN * MODES, PAIR)
    spread = dot(filtered, tab["inv3"][...]).astype(BF16)
    level = jnp.zeros((GRID, GRID), F32)
    for k in range(KERN):
        one = spread[k * MODES : (k + 1) * MODES]
        real, imag = one[:, :GRID], one[:, GRID:]
        rotated = jnp.concatenate(
            [one, jnp.concatenate([-imag, real], 1)], 0
        )
        field = dot(tab["lift"][...], rotated)
        fields[k] = field.astype(BF16)
        level += field[:, :GRID] * field[:, :GRID] + field[:, GRID:] * field[:, GRID:]
    across = dot(level.astype(BF16), tab["down"][...]).astype(BF16)
    core = dot(tab["up"][...], across)
    printed = above_half(STEEPNESS * (core - THRESHOLD))
    pull = (4.0 * STEEPNESS) * (printed + (0.5 - goal.astype(F32))) * (0.25 - printed * printed)
    if counted is not None:
        pull = jnp.where(counted, pull, 0.0)
    pull = dot(pull.astype(BF16), tab["up"][...]).astype(BF16)
    pull = dot(tab["down"][...], pull)
    pull = pull.astype(BF16)
    both = jnp.concatenate([pull, pull], 1)
    scaled = (fields[...] * both[None]).reshape(KERN * GRID, 2 * GRID)
    back = dot(scaled, tab["adj"][...]).astype(BF16)
    sum_real = jnp.zeros((MODES, PAIR), F32)
    sum_imag = jnp.zeros((MODES, PAIR), F32)
    for k in range(0, KERN, 2):
        one, two = back[k * GRID : (k + 1) * GRID], back[(k + 1) * GRID : (k + 2) * GRID]
        upper = jnp.concatenate([one[:, :PAIR], two[:, :PAIR]], 1)
        lower = jnp.concatenate([one[:, PAIR:], two[:, PAIR:]], 1)
        modes = dot(tab["fold"][...], jnp.concatenate([upper, lower], 0))
        for n in range(2):
            half = modes[:, n * PAIR : (n + 1) * PAIR]
            sum_real += resp_real[k + n] * half
            sum_imag += resp_imag[k + n] * half
    return (sum_real - turned(sum_imag)).astype(BF16)


def core_gradient(modes, tab, low_row, rows, low_col, cols):
    part = jnp.concatenate(
        [
            tab["invc"][:, low_col : low_col + cols],
            tab["invc"][:, TILE + low_col : TILE + low_col + cols],
        ],
        1,
    )
    partial = dot(modes, part).astype(BF16)
    stacked = jnp.concatenate([partial[:, :cols], partial[:, cols:]], 0)
    return dot(tab["rowc"][low_row : low_row + rows], stacked)


def kernel(sizes, weight, *refs):
    count = 3 + len(NAMES)
    far, (none1, none2), refs = refs[:count], refs[count : count + 2], refs[count + 2 :]
    out, near, refs = refs[0], refs[1 : 1 + count], refs[1 + count :]
    mask, target, modes = near[:3]
    tab = dict(zip(NAMES, near[3:]))
    (
        resp_real, resp_imag, fields, first, soft,
        out1, in1, out2, in2, out3, in3, goals, base1, base2,
        send1, recv1, send2, recv2, send3, recv3, send_goal, recv_goal, load, none_sem,
    ) = refs
    n_row, n_col = sizes
    row, col = lax.axis_index("row"), lax.axis_index("col")

    def there(di, dj):
        ok_row = {-1: row >= 1, 0: row >= 0, 1: row < n_row - 1}[di]
        ok_col = {-1: col >= 1, 0: col >= 0, 1: col < n_col - 1}[dj]
        return jnp.logical_and(ok_row, ok_col)

    def place(di, dj):
        return {"row": row + di, "col": col + dj}

    order = ("mask", "col1", "row1", "target", "modes") + NAMES[2:]
    slot = {"mask": 0, "target": 1, "modes": 2} | {n: 3 + k for k, n in enumerate(NAMES)}
    loads = {
        name: pltpu.make_async_copy(far[slot[name]], near[slot[name]], load.at[slot[name]])
        for name in order
    }
    for name in order:
        loads[name].start()
    edges = [(row == 0), (row == n_row - 1), (col == 0), (col == n_col - 1)]
    up, down, left, right = [edge.astype(jnp.int32) for edge in edges]
    load_none1 = pltpu.make_async_copy(
        none1.at[up + 2 * down + 4 * left + 8 * right], base1, none_sem.at[0]
    )
    load_none2 = pltpu.make_async_copy(none2.at[down + 2 * right], base2, none_sem.at[1])
    load_none1.start()
    load_none2.start()

    barrier = pltpu.get_barrier_semaphore()
    for di, dj in AROUND:

        @pl.when(there(di, dj))
        def _():
            pl.semaphore_signal(barrier, inc=1, device_id=place(di, dj), device_id_type=MESH)

    def copies(ways, source, landing, send, recv):
        return [
            pltpu.make_async_remote_copy(
                src_ref=source(n),
                dst_ref=landing.at[n],
                send_sem=send.at[n],
                recv_sem=recv.at[n],
                device_id=place(di, dj),
                device_id_type=MESH,
            )
            for n, (di, dj) in enumerate(ways)
        ]

    def start(ways, group):
        for (di, dj), copy in zip(ways, group):

            @pl.when(there(di, dj))
            def _():
                copy.start()

    def arrive(ways, group):
        for (di, dj), copy in zip(ways, group):

            @pl.when(there(-di, -dj))
            def _():
                copy.wait_recv()

    def sent(ways, group):
        for (di, dj), copy in zip(ways, group):

            @pl.when(there(di, dj))
            def _():
                copy.wait_send()

    def blank(ways, landing):
        for n, (di, dj) in enumerate(ways):

            @pl.when(jnp.logical_not(there(-di, -dj)))
            def _():
                landing[n] = jnp.zeros(landing.shape[1:], landing.dtype)

    corner = {-1: 0, 0: HALF}
    copies1 = copies(AROUND, lambda n: out1.at[n], in1, send1, recv1)
    copies2 = copies(BACK, lambda n: out2.at[n], in2, send2, recv2)
    copies3 = copies(AHEAD, lambda n: out3, in3, send3, recv3)
    copies_goal = copies(
        BACK,
        lambda n: target.at[
            pl.ds(corner[BACK[n][0]], HALF), pl.ds(corner[BACK[n][1]], HALF)
        ],
        goals,
        send_goal,
        recv_goal,
    )

    for name in ("mask", "col1", "row1"):
        loads[name].wait()
    own_soft = above_half(mask[...])
    soft[...] = own_soft
    parts = spectrum_parts(own_soft.astype(BF16), tab["col1"], tab["row1"], 3)

    def part_of(parts, di, dj):
        return parts[(di + 1) * MODES : (di + 2) * MODES, (dj + 1) * PAIR : (dj + 2) * PAIR]

    for n, (di, dj) in enumerate(AROUND):
        out1[n] = part_of(parts, di, dj).astype(out1.dtype)
    rows_around = 1 + (row >= 1).astype(jnp.int32) + (row < n_row - 1).astype(jnp.int32)
    cols_around = 1 + (col >= 1).astype(jnp.int32) + (col < n_col - 1).astype(jnp.int32)
    pl.semaphore_wait(barrier, rows_around * cols_around - 1)
    start(AROUND, copies1)

    blank(AROUND, in1)
    blank(BACK, in2)
    blank(AHEAD, in3)
    blank(BACK, goals)
    loads["modes"].wait()
    for k in range(KERN):
        pair = modes[k] * jnp.sqrt(jnp.full((MODES, PAIR), weight[k], F32))
        other = pltpu.roll(pair, MODES, 1)
        resp_real[k] = jnp.where(low_half(), pair, other)
        resp_imag[k] = jnp.where(low_half(), other, pair)

    for name in ("target",) + NAMES[2:]:
        loads[name].wait()
    load_none1.wait()
    load_none2.wait()
    arrive(AROUND, copies1)
    start(BACK, copies_goal)
    spec = part_of(parts, 0, 0) + base1[...]
    for n in range(len(AROUND)):
        spec += in1[n].astype(F32)
    found = adjoint_modes(spec, target[...], None, resp_real, resp_imag, fields, tab)
    slope = core_gradient(found, tab, 0, TILE, 0, TILE)
    own_soft = soft[...]
    new = mask[...] - (STEP / (WIN * WIN)) * (slope * (0.25 - own_soft * own_soft))
    first[...] = new

    own_soft = above_half(new)
    soft[...] = own_soft
    parts = spectrum_parts(own_soft.astype(BF16), tab["col2"], tab["row2"], 2)
    for n, (di, dj) in enumerate(BACK):
        out2[n] = part_of(parts, di, dj).astype(out2.dtype)
    start(BACK, copies2)
    arrive(BACK, copies_goal)
    goal = jnp.concatenate(
        [
            jnp.concatenate([target[HALF:, HALF:], goals[2]], 1),
            jnp.concatenate([goals[1], goals[0]], 1),
        ],
        0,
    )
    row_at = lax.broadcasted_iota(jnp.int32, (TILE, TILE), 0)
    col_at = lax.broadcasted_iota(jnp.int32, (TILE, TILE), 1)
    row_end = jnp.where(row < n_row - 1, TILE, HALF)
    col_end = jnp.where(col < n_col - 1, TILE, HALF)
    counted = jnp.logical_and(row_at < row_end, col_at < col_end)
    arrive(BACK, copies2)
    spec = part_of(parts, 0, 0) + base2[...]
    for n in range(len(BACK)):
        spec += in2[n].astype(F32)
    found = adjoint_modes(spec, goal, counted, resp_real, resp_imag, fields, tab)
    out3[...] = found
    start(AHEAD, copies3)

    def finish(modes, di, dj):
        at_row, at_col = (0 if di else HALF), (0 if dj else HALF)
        slope = core_gradient(modes, tab, HALF - at_row, HALF, HALF - at_col, HALF)
        here = (slice(at_row, at_row + HALF), slice(at_col, at_col + HALF))
        own_soft, before = soft[here], first[here]
        after = before - (STEP / (WIN * WIN)) * (slope * (0.25 - own_soft * own_soft))
        out[here] = jnp.where(there(-di, -dj), after, before)

    finish(found, 0, 0)
    arrive(AHEAD, copies3)
    for n, (di, dj) in enumerate(AHEAD):
        finish(in3[n], di, dj)

    sent(AROUND, copies1)
    sent(BACK, copies_goal)
    sent(BACK, copies2)
    sent(AHEAD, copies3)


def solution(mesh):
    sizes = (mesh.shape["row"], mesh.shape["col"])
    made = tables()
    held = [made[name] for name in NAMES + ABSENT]

    def per_device(mask_param, target, kernel_modes, kernel_weight):
        vmem = pl.BlockSpec(memory_space=pltpu.VMEM)
        message = (MODES, PAIR)
        return pl.pallas_call(
            functools.partial(kernel, sizes),
            out_shape=jax.ShapeDtypeStruct((TILE, TILE), F32),
            in_specs=[pl.BlockSpec(memory_space=pltpu.SMEM)]
            + [pl.BlockSpec(memory_space=pltpu.HBM)] * (3 + len(held)),
            out_specs=vmem,
            scratch_shapes=[
                pltpu.VMEM((TILE, TILE), F32),
                pltpu.VMEM((TILE, TILE), BF16),
                pltpu.VMEM((KERN,) + message, F32),
            ]
            + [pltpu.VMEM(made[name].shape, BF16) for name in NAMES]
            + [
                pltpu.VMEM((KERN,) + message, F32),
                pltpu.VMEM((KERN,) + message, F32),
                pltpu.VMEM((KERN, GRID, 2 * GRID), BF16),
                pltpu.VMEM((TILE, TILE), F32),
                pltpu.VMEM((TILE, TILE), F32),
                pltpu.VMEM((len(AROUND),) + message, BF16),
                pltpu.VMEM((len(AROUND),) + message, BF16),
                pltpu.VMEM((len(BACK),) + message, BF16),
                pltpu.VMEM((len(BACK),) + message, BF16),
                pltpu.VMEM(message, BF16),
                pltpu.VMEM((len(AHEAD),) + message, BF16),
                pltpu.VMEM((len(BACK), HALF, HALF), BF16),
                pltpu.VMEM(message, F32),
                pltpu.VMEM(message, F32),
            ]
            + [
                pltpu.SemaphoreType.DMA((count,))
                for count in (8, 8, 3, 3, 3, 3, 3, 3, 3 + len(NAMES), 2)
            ],
            compiler_params=pltpu.CompilerParams(
                collective_id=0, has_side_effects=True, vmem_limit_bytes=60 * 1024 * 1024
            ),
            cost_estimate=pl.CostEstimate(
                flops=1_000_000_000, bytes_accessed=3_000_000, transcendentals=300_000
            ),
        )(kernel_weight, mask_param, target, kernel_modes, *[jnp.asarray(t) for t in held])

    spread = P(("grp", "row"), "col")
    return jax.shard_map(
        per_device, mesh=mesh, in_specs=(spread, spread, P(), P()), out_specs=spread,
        check_vma=False,
    )
```

profile of v0, /device:TPU:17, one launch (start us, length us, event | category | flops | bytes accessed | tf_op | source)
XLA Modules:
  0.0 20.2 jit_solution(13066126876732795029)
XLA Ops:
  0.0 18.5 %shard_map.172 = f32[256,256]{1,0:T(8,128)} custom-call(f32[12]{0:T(128)} %weight.1, f32[256,256]{1,0:T(8,128)} %refs_0_.1, bf16[256,256]{1,0:T(8,128)(2,1)} %refs_1_.1, f32[12,64,128]{2,1,0:T(8,128)} %refs_2_.1, bf16[256,768]{1,0:T(8,128)(2,1)} %constant.28.clone.refs_3_, bf16[192,512]{1,0:T(8,128)(2,1)} %constant.29.clone.refs_4_, ...), custom_call_target="tpu_custom_call" | custom-call | flops 1000000000 | bytes 3000000 | tf_op jit(solution)/shard_map/pallas_call | solution.py:392
  18.6 1.7 %copy.20 = f32[256,256]{1,0:T(8,128)} copy(f32[256,256]{1,0:T(8,128)} %shard_map.172) | data formatting | bytes 524288
where the time goes:
time: 20.4 us; the launch traced here: 20.2 us
  Pallas kernels  18.5 us (91%)
  local copies, waits for them, and re-layouts  1.67 us (8%)
    pallas_call x1, Pallas kernels, per_device(): pl.pallas_call(functools.partial(kernel, sizes), out_shape=jax.ShapeDtype...  18.5 us
    unnamed x1, local copies, waits for them, and re-layouts  1.67 us

commit v1 on v0

--- a/solution.py
+++ b/solution.py
@@ -17,6 +17,7 @@
 WIN = 384
 GRID = 128
 PAIR = 2 * MODES
+GROUP = 4
 
 STEEPNESS = 4.0
 THRESHOLD = 0.4
@@ -140,19 +141,23 @@
 
 
 def adjoint_modes(spec, goal, counted, resp_real, resp_imag, fields, tab):
-    filtered = resp_real[...] * spec[None] + resp_imag[...] * turned(spec)[None]
-    filtered = filtered.astype(BF16).reshape(KERN * MODES, PAIR)
-    spread = dot(filtered, tab["inv3"][...]).astype(BF16)
+    other = turned(spec)
+    lifted = []
+    for k in range(0, KERN, 2):
+        pair = []
+        for n in (k, k + 1):
+            filtered = resp_real[n] * spec + resp_imag[n] * other
+            rotated = resp_real[n] * other - resp_imag[n] * spec
+            pair.append(jnp.concatenate([filtered.astype(BF16), rotated.astype(BF16)], 0))
+        both = dot(tab["lift"][...], jnp.concatenate(pair, 1)).astype(BF16)
+        lifted += [both[:, :PAIR], both[:, PAIR:]]
     level = jnp.zeros((GRID, GRID), F32)
-    for k in range(KERN):
-        one = spread[k * MODES : (k + 1) * MODES]
-        real, imag = one[:, :GRID], one[:, GRID:]
-        rotated = jnp.concatenate(
-            [one, jnp.concatenate([-imag, real], 1)], 0
-        )
-        field = dot(tab["lift"][...], rotated)
-        fields[k] = field.astype(BF16)
-        level += field[:, :GRID] * field[:, :GRID] + field[:, GRID:] * field[:, GRID:]
+    for k in range(0, KERN, GROUP):
+        group = dot(jnp.concatenate(lifted[k : k + GROUP], 0), tab["inv3"][...])
+        for n in range(GROUP):
+            field = group[n * GRID : (n + 1) * GRID]
+            fields[k + n] = field.astype(BF16)
+            level += field[:, :GRID] * field[:, :GRID] + field[:, GRID:] * field[:, GRID:]
     across = dot(level.astype(BF16), tab["down"][...]).astype(BF16)
     core = dot(tab["up"][...], across)
     printed = above_half(STEEPNESS * (core - THRESHOLD))
@@ -202,6 +207,7 @@
         resp_real, resp_imag, fields, first, soft,
         out1, in1, out2, in2, out3, in3, goals, base1, base2,
         send1, recv1, send2, recv2, send3, recv3, send_goal, recv_goal, load, none_sem,
+        moved, save,
     ) = refs
     n_row, n_col = sizes
     row, col = lax.axis_index("row"), lax.axis_index("col")
@@ -213,6 +219,13 @@
 
     def place(di, dj):
         return {"row": row + di, "col": col + dj}
+
+    barrier = pltpu.get_barrier_semaphore()
+    for di, dj in AROUND:
+
+        @pl.when(there(di, dj))
+        def _():
+            pl.semaphore_signal(barrier, inc=1, device_id=place(di, dj), device_id_type=MESH)
 
     order = ("mask", "col1", "row1", "target", "modes") + NAMES[2:]
     slot = {"mask": 0, "target": 1, "modes": 2} | {n: 3 + k for k, n in enumerate(NAMES)}
@@ -230,13 +243,6 @@
     load_none2 = pltpu.make_async_copy(none2.at[down + 2 * right], base2, none_sem.at[1])
     load_none1.start()
     load_none2.start()
-
-    barrier = pltpu.get_barrier_semaphore()
-    for di, dj in AROUND:
-
-        @pl.when(there(di, dj))
-        def _():
-            pl.semaphore_signal(barrier, inc=1, device_id=place(di, dj), device_id_type=MESH)
 
     def copies(ways, source, landing, send, recv):
         return [
@@ -362,23 +368,34 @@
     out3[...] = found
     start(AHEAD, copies3)
 
-    def finish(modes, di, dj):
+    quarters = ((0, 0),) + AHEAD
+
+    def save_quarter(n):
+        di, dj = quarters[n]
+        here = (pl.ds(0 if di else HALF, HALF), pl.ds(0 if dj else HALF, HALF))
+        return pltpu.make_async_copy(moved.at[n], out.at[here], save.at[n])
+
+    def finish(n, modes):
+        di, dj = quarters[n]
         at_row, at_col = (0 if di else HALF), (0 if dj else HALF)
         slope = core_gradient(modes, tab, HALF - at_row, HALF, HALF - at_col, HALF)
-        here = (slice(at_row, at_row + HALF), slice(at_col, at_col + HALF))
-        own_soft, before = soft[here], first[here]
+        own_soft = soft[at_row : at_row + HALF, at_col : at_col + HALF]
+        before = first[at_row : at_row + HALF, at_col : at_col + HALF]
         after = before - (STEP / (WIN * WIN)) * (slope * (0.25 - own_soft * own_soft))
-        out[here] = jnp.where(there(-di, -dj), after, before)
-
-    finish(found, 0, 0)
+        moved[n] = jnp.where(there(-di, -dj), after, before)
+        save_quarter(n).start()
+
+    finish(0, found)
     arrive(AHEAD, copies3)
-    for n, (di, dj) in enumerate(AHEAD):
-        finish(in3[n], di, dj)
+    for n in range(len(AHEAD)):
+        finish(n + 1, in3[n])
 
     sent(AROUND, copies1)
     sent(BACK, copies_goal)
     sent(BACK, copies2)
     sent(AHEAD, copies3)
+    for n in range(len(quarters)):
+        save_quarter(n).wait()
 
 
 def solution(mesh):
@@ -387,14 +404,13 @@
     held = [made[name] for name in NAMES + ABSENT]
 
     def per_device(mask_param, target, kernel_modes, kernel_weight):
-        vmem = pl.BlockSpec(memory_space=pltpu.VMEM)
         message = (MODES, PAIR)
         return pl.pallas_call(
             functools.partial(kernel, sizes),
             out_shape=jax.ShapeDtypeStruct((TILE, TILE), F32),
             in_specs=[pl.BlockSpec(memory_space=pltpu.SMEM)]
             + [pl.BlockSpec(memory_space=pltpu.HBM)] * (3 + len(held)),
-            out_specs=vmem,
+            out_specs=pl.BlockSpec(memory_space=pltpu.HBM),
             scratch_shapes=[
                 pltpu.VMEM((TILE, TILE), F32),
                 pltpu.VMEM((TILE, TILE), BF16),
@@ -420,7 +436,8 @@
             + [
                 pltpu.SemaphoreType.DMA((count,))
                 for count in (8, 8, 3, 3, 3, 3, 3, 3, 3 + len(NAMES), 2)
-            ],
+            ]
+            + [pltpu.VMEM((4, HALF, HALF), F32), pltpu.SemaphoreType.DMA((4,))],
             compiler_params=pltpu.CompilerParams(
                 collective_id=0, has_side_effects=True, vmem_limit_bytes=60 * 1024 * 1024
             ),

time: 20.4 us -> 20.4 us (level)
  no operation moved by 1% of the time
where the time goes in v1:
time: 20.4 us; the launch traced here: 20.3 us
  Pallas kernels  18.6 us (91%)
  local copies, waits for them, and re-layouts  1.67 us (8%)
    pallas_call x1, Pallas kernels, per_device(): pl.pallas_call(functools.partial(kernel, sizes), out_shape=jax.ShapeDtype...  18.6 us
    unnamed x1, local copies, waits for them, and re-layouts  1.67 us

profile of v1, /device:TPU:17, one launch (start us, length us, event | category | flops | bytes accessed | tf_op | source)
XLA Modules:
  0.0 20.3 jit_solution(3103092124696004071)
XLA Ops:
  0.0 18.6 %shard_map.172 = f32[256,256]{1,0:T(8,128)} custom-call(f32[12]{0:T(128)} %weight.1, f32[256,256]{1,0:T(8,128)} %refs_0_.1, bf16[256,256]{1,0:T(8,128)(2,1)} %refs_1_.1, f32[12,64,128]{2,1,0:T(8,128)} %refs_2_.1, bf16[256,768]{1,0:T(8,128)(2,1)} %constant.28.clone.refs_3_, bf16[192,512]{1,0:T(8,128)(2,1)} %constant.29.clone.refs_4_, ...), custom_call_target="tpu_custom_call" | custom-call | flops 1000000000 | bytes 3000000 | tf_op jit(solution)/shard_map/pallas_call | solution.py:408
  18.6 1.7 %copy.20 = f32[256,256]{1,0:T(8,128)} copy(f32[256,256]{1,0:T(8,128)} %shard_map.172) | data formatting | bytes 524288

commit v2 on v1

--- a/solution.py
+++ b/solution.py
@@ -137,7 +137,10 @@
     wide = PAIR * count
     half = dot(wire, col[...]).astype(BF16)
     stacked = jnp.concatenate([half[:, :wide], half[:, wide:]], 0)
-    return dot(row[...], stacked) * (1.0 / (WIN * WIN))
+    scale = 1.0 / (WIN * WIN)
+    return [
+        dot(row[n * MODES : (n + 1) * MODES], stacked) * scale for n in range(count)
+    ]
 
 
 def adjoint_modes(spec, goal, counted, resp_real, resp_imag, fields, tab):
@@ -168,12 +171,12 @@
     pull = dot(tab["down"][...], pull)
     pull = pull.astype(BF16)
     both = jnp.concatenate([pull, pull], 1)
-    scaled = (fields[...] * both[None]).reshape(KERN * GRID, 2 * GRID)
-    back = dot(scaled, tab["adj"][...]).astype(BF16)
     sum_real = jnp.zeros((MODES, PAIR), F32)
     sum_imag = jnp.zeros((MODES, PAIR), F32)
     for k in range(0, KERN, 2):
-        one, two = back[k * GRID : (k + 1) * GRID], back[(k + 1) * GRID : (k + 2) * GRID]
+        scaled = jnp.concatenate([fields[k] * both, fields[k + 1] * both], 0)
+        back = dot(scaled, tab["adj"][...]).astype(BF16)
+        one, two = back[:GRID], back[GRID:]
         upper = jnp.concatenate([one[:, :PAIR], two[:, :PAIR]], 1)
         lower = jnp.concatenate([one[:, PAIR:], two[:, PAIR:]], 1)
         modes = dot(tab["fold"][...], jnp.concatenate([upper, lower], 0))
@@ -233,7 +236,7 @@
         name: pltpu.make_async_copy(far[slot[name]], near[slot[name]], load.at[slot[name]])
         for name in order
     }
-    for name in order:
+    for name in order[:3]:
         loads[name].start()
     edges = [(row == 0), (row == n_row - 1), (col == 0), (col == n_col - 1)]
     up, down, left, right = [edge.astype(jnp.int32) for edge in edges]
@@ -243,6 +246,8 @@
     load_none2 = pltpu.make_async_copy(none2.at[down + 2 * right], base2, none_sem.at[1])
     load_none1.start()
     load_none2.start()
+    for name in order[3:]:
+        loads[name].start()
 
     def copies(ways, source, landing, send, recv):
         return [
@@ -306,7 +311,7 @@
     parts = spectrum_parts(own_soft.astype(BF16), tab["col1"], tab["row1"], 3)
 
     def part_of(parts, di, dj):
-        return parts[(di + 1) * MODES : (di + 2) * MODES, (dj + 1) * PAIR : (dj + 2) * PAIR]
+        return parts[di + 1][:, (dj + 1) * PAIR : (dj + 2) * PAIR]
 
     for n, (di, dj) in enumerate(AROUND):
         out1[n] = part_of(parts, di, dj).astype(out1.dtype)

time: 20.4 us -> 21.9 us (1.074)
  Pallas kernels: 18.6 us -> 20 us
    pallas_call x1, Pallas kernels: 18.6 us -> 20 us  [per_device(): pl.pallas_call(functools.partial(kernel, sizes), out_shape=jax.ShapeDtype...]
where the time goes in v2:
time: 21.9 us; the launch traced here: 21.7 us
  Pallas kernels  20 us (91%)
  local copies, waits for them, and re-layouts  1.67 us (8%)
    pallas_call x1, Pallas kernels, per_device(): pl.pallas_call(functools.partial(kernel, sizes), out_shape=jax.ShapeDtype...  20 us
    unnamed x1, local copies, waits for them, and re-layouts  1.67 us

profile of v2, /device:TPU:17, one launch (start us, length us, event | category | flops | bytes accessed | tf_op | source)
XLA Modules:
  0.0 21.7 jit_solution(4247026537127141926)
XLA Ops:
  0.0 20.0 %shard_map.172 = f32[256,256]{1,0:T(8,128)} custom-call(f32[12]{0:T(128)} %weight.1, f32[256,256]{1,0:T(8,128)} %refs_0_.1, bf16[256,256]{1,0:T(8,128)(2,1)} %refs_1_.1, f32[12,64,128]{2,1,0:T(8,128)} %refs_2_.1, bf16[256,768]{1,0:T(8,128)(2,1)} %constant.28.clone.refs_3_, bf16[192,512]{1,0:T(8,128)(2,1)} %constant.29.clone.refs_4_, ...), custom_call_target="tpu_custom_call" | custom-call | flops 1000000000 | bytes 3000000 | tf_op jit(solution)/shard_map/pallas_call | solution.py:413
  20.0 1.7 %copy.20 = f32[256,256]{1,0:T(8,128)} copy(f32[256,256]{1,0:T(8,128)} %shard_map.172) | data formatting | bytes 524288

commit v3 on v1

--- a/solution.py
+++ b/solution.py
@@ -17,7 +17,6 @@
 WIN = 384
 GRID = 128
 PAIR = 2 * MODES
-GROUP = 4
 
 STEEPNESS = 4.0
 THRESHOLD = 0.4
@@ -142,22 +141,17 @@
 
 def adjoint_modes(spec, goal, counted, resp_real, resp_imag, fields, tab):
     other = turned(spec)
-    lifted = []
-    for k in range(0, KERN, 2):
-        pair = []
-        for n in (k, k + 1):
-            filtered = resp_real[n] * spec + resp_imag[n] * other
-            rotated = resp_real[n] * other - resp_imag[n] * spec
-            pair.append(jnp.concatenate([filtered.astype(BF16), rotated.astype(BF16)], 0))
-        both = dot(tab["lift"][...], jnp.concatenate(pair, 1)).astype(BF16)
-        lifted += [both[:, :PAIR], both[:, PAIR:]]
-    level = jnp.zeros((GRID, GRID), F32)
-    for k in range(0, KERN, GROUP):
-        group = dot(jnp.concatenate(lifted[k : k + GROUP], 0), tab["inv3"][...])
-        for n in range(GROUP):
-            field = group[n * GRID : (n + 1) * GRID]
-            fields[k + n] = field.astype(BF16)
-            level += field[:, :GRID] * field[:, :GRID] + field[:, GRID:] * field[:, GRID:]
+    pairs = []
+    for k in range(KERN):
+        filtered = resp_real[k] * spec + resp_imag[k] * other
+        rotated = resp_real[k] * other - resp_imag[k] * spec
+        pairs.append(jnp.concatenate([filtered.astype(BF16), rotated.astype(BF16)], 0))
+    lifted = dot(tab["lift"][...], jnp.concatenate(pairs, 1)).astype(BF16)
+    lifted = [lifted[:, k * PAIR : (k + 1) * PAIR] for k in range(KERN)]
+    field = dot(jnp.concatenate(lifted, 0), tab["inv3"][...]).reshape(KERN, GRID, 2 * GRID)
+    fields[...] = field.astype(BF16)
+    power = jnp.sum(field * field, 0)
+    level = power[:, :GRID] + power[:, GRID:]
     across = dot(level.astype(BF16), tab["down"][...]).astype(BF16)
     core = dot(tab["up"][...], across)
     printed = above_half(STEEPNESS * (core - THRESHOLD))
@@ -172,15 +166,15 @@
     back = dot(scaled, tab["adj"][...]).astype(BF16)
     sum_real = jnp.zeros((MODES, PAIR), F32)
     sum_imag = jnp.zeros((MODES, PAIR), F32)
-    for k in range(0, KERN, 2):
-        one, two = back[k * GRID : (k + 1) * GRID], back[(k + 1) * GRID : (k + 2) * GRID]
-        upper = jnp.concatenate([one[:, :PAIR], two[:, :PAIR]], 1)
-        lower = jnp.concatenate([one[:, PAIR:], two[:, PAIR:]], 1)
-        modes = dot(tab["fold"][...], jnp.concatenate([upper, lower], 0))
-        for n in range(2):
-            half = modes[:, n * PAIR : (n + 1) * PAIR]
-            sum_real += resp_real[k + n] * half
-            sum_imag += resp_imag[k + n] * half
+    stacked = []
+    for k in range(KERN):
+        one = back[k * GRID : (k + 1) * GRID]
+        stacked.append(jnp.concatenate([one[:, :PAIR], one[:, PAIR:]], 0))
+    modes = dot(tab["fold"][...], jnp.concatenate(stacked, 1))
+    for k in range(KERN):
+        one = modes[:, k * PAIR : (k + 1) * PAIR]
+        sum_real += resp_real[k] * one
+        sum_imag += resp_imag[k] * one
     return (sum_real - turned(sum_imag)).astype(BF16)
 
 

time: 20.4 us -> 20.4 us (level)
  no operation moved by 1% of the time
where the time goes in v3:
time: 20.4 us; the launch traced here: 20.3 us
  Pallas kernels  18.6 us (91%)
  local copies, waits for them, and re-layouts  1.67 us (8%)
    pallas_call x1, Pallas kernels, per_device(): pl.pallas_call(functools.partial(kernel, sizes), out_shape=jax.ShapeDtype...  18.6 us
    unnamed x1, local copies, waits for them, and re-layouts  1.67 us

profile of v3, /device:TPU:17, one launch (start us, length us, event | category | flops | bytes accessed | tf_op | source)
XLA Modules:
  0.0 20.3 jit_solution(16432516065595060094)
XLA Ops:
  0.0 18.6 %shard_map.172 = f32[256,256]{1,0:T(8,128)} custom-call(f32[12]{0:T(128)} %weight.1, f32[256,256]{1,0:T(8,128)} %refs_0_.1, bf16[256,256]{1,0:T(8,128)(2,1)} %refs_1_.1, f32[12,64,128]{2,1,0:T(8,128)} %refs_2_.1, bf16[256,768]{1,0:T(8,128)(2,1)} %constant.28.clone.refs_3_, bf16[192,512]{1,0:T(8,128)(2,1)} %constant.29.clone.refs_4_, ...), custom_call_target="tpu_custom_call" | custom-call | flops 1000000000 | bytes 3000000 | tf_op jit(solution)/shard_map/pallas_call | solution.py:402
  18.6 1.7 %copy.20 = f32[256,256]{1,0:T(8,128)} copy(f32[256,256]{1,0:T(8,128)} %shard_map.172) | data formatting | bytes 524288
